TPU v7x, 512 devices: a whole 4x4x16 slice. The times are simulated.
512 devices in a mesh: row: 8 (over y, z_hi), col: 64 (over z_lo, x, core).
Axes of the slice: x: 4, y: 4, z: 16 (z_hi: 2, z_lo: 8; z = z_hi * 8 + z_lo), core: 2. Of those that a mesh axis runs over, the one named last changes fastest.
Arguments:
- side_a: float32 [64, 8192], P('row', 'col'), may hold values from -6 to 6
- side_b: float32 [2048, 8192], P('col', 'row'), may hold values from -6 to 6
- pair_grad: float32 [64, 2048, 128], P('row', 'col'), may hold values from -6 to 6
- out_weight: float32 [1024, 128], replicated, may hold values from -0.1875 to 0.1875
Outputs:
- grad_a: float32 [64, 8192], P('row', 'col')
- grad_b: float32 [2048, 8192], P('col', 'row')
- grad_weight: float32 [1024, 128], replicated
- grad_bias: float32 [128], replicated
All inputs are finite; a program needn't handle non-finite values.
Results may differ from a plain program's by a relative error of at most 0.00013.
Values sent between devices are 32-bit elements; how exact they have to be, the bound alone decides.
A program may use at most 64 MiB of HBM per device.

v0:
```python
import jax
import jax.numpy as jnp
from jax import lax
from jax.sharding import PartitionSpec as P

S = 256
C = 32
P_SIZE = 128


def local(side_a, side_b, pair_grad, out_weight):
    high = lax.Precision.HIGHEST
    rows = pair_grad.shape[0]
    cols = pair_grad.shape[1]
    left = lax.all_gather(side_a, "col", axis=1, tiled=True).reshape(rows, S, C)
    right = lax.all_gather(side_b, "row", axis=1, tiled=True).reshape(cols, S, C)
    left_flat = jnp.transpose(left, (0, 2, 1)).reshape(rows * C, S)
    right_flat = jnp.transpose(right, (1, 0, 2)).reshape(S, cols * C)
    flat_pair = pair_grad.reshape(rows * cols, P_SIZE)
    grad_outer = jnp.dot(flat_pair, out_weight.T, precision=high)
    grad_tile = jnp.transpose(grad_outer.reshape(rows, cols, C, C), (0, 2, 1, 3)).reshape(
        rows * C, cols * C
    )
    left_grad = jnp.dot(grad_tile, right_flat.T, precision=high) / S
    left_part = jnp.transpose(left_grad.reshape(rows, C, S), (0, 2, 1)).reshape(rows, S * C)
    right_grad = jnp.dot(left_flat.T, grad_tile, precision=high) / S
    right_part = jnp.transpose(right_grad.reshape(S, cols, C), (1, 0, 2)).reshape(cols, S * C)
    left_total = lax.psum(left_part, "col")
    right_total = lax.psum(right_part, "row")
    left_width = side_a.shape[1]
    right_width = side_b.shape[1]
    grad_a = lax.dynamic_slice_in_dim(left_total, lax.axis_index("col") * left_width, left_width, 1)
    grad_b = lax.dynamic_slice_in_dim(
        right_total, lax.axis_index("row") * right_width, right_width, 1
    )
    outer = jnp.dot(left_flat, right_flat, precision=high) / S
    outer = jnp.transpose(outer.reshape(rows, C, cols, C), (0, 2, 1, 3)).reshape(rows * cols, C * C)
    weight_part = jnp.dot(outer.T, flat_pair, precision=high)
    bias_part = jnp.sum(flat_pair, axis=0)
    weight_sums = lax.psum((weight_part, bias_part), ("row", "col"))
    return (grad_a, grad_b, weight_sums[0], weight_sums[1])


def solution(mesh):
    in_specs = (P("row", "col"), P("col", "row"), P("row", "col", None), P())
    out_specs = (P("row", "col"), P("col", "row"), P(), P())
    return jax.shard_map(local, mesh=mesh, in_specs=in_specs, out_specs=out_specs, check_vma=False)
```

profile of v0, /device:TPU:4, one launch (start us, length us, event | category | flops | bytes accessed | tf_op | source)
XLA Modules:
  0.0 1648.9 jit_solution(14450162567662222692)
XLA Ops:
  7.2 0.0 all-gather.2.cloned.1.call-start
  7.2 0.7 all-gather.2.cloned.1.call-update
  7.9 0.0 all-reduce.6.cloned.1.call-start
  8.0 0.3 copy-done
  8.2 5.9 convolution_bitcast_fusion
  14.1 3.7 reshape.48
  17.9 119.1 %all_gather.7 = f32[8,8192]{1,0:T(8,128)S(1)} all-gather(f32[8,128]{1,0:T(8,128)S(1)} %copy-done.2), channel_id=1, replica_groups=mesh['row'=8,'col'=64] {'col'}, dimensions={1}, use_global_device_ids=true | all-gather | bytes 266240 | tf_op jit(solution)/shard_map/all_gather | solution.py:15
  137.0 0.3 reshape.53
  137.3 0.3 copy.12
  137.6 1.8 convolution_multiply_fusion.1
  139.5 2.6 copy.13
  142.1 4.4 reshape.56
  146.5 0.2 all-reduce.4.cloned.1.call-start
  146.8 3.7 reshape.49
  150.5 2.8 copy.10
  153.3 1.0 convolution_multiply_fusion.2
  154.4 0.3 copy.11
  154.7 1.2 reshape.52
  155.9 1.0 convolution_multiply_fusion
  157.0 2.7 reshape.57
  159.7 6.5 copy.17
  166.2 3.8 reshape.58
  170.0 0.0 all-reduce.8.cloned.1.call-start
  170.1 2.6 fusion.1
  172.7 0.1 reduce_sum.9
  172.8 158.6 %psum.31 = f32[128]{0:T(128)} all-reduce(f32[128]{0:T(128)S(1)} %reduce_sum.9), channel_id=1, replica_groups=mesh['row'=8,'col'=64] {'row','col'}, use_global_device_ids=true, to_apply=%region_4.0 | all-reduce | flops 128 | bytes 1024 | tf_op jit(solution)/shard_map/psum | solution.py:40
  331.4 64.2 %all-reduce.6.cloned.1.call-done = f32[32,8192]{1,0:T(8,128)} async-done(((f32[32,8192]{1,0:T(8,128)}), f32[32,8192]{1,0:T(8,128)}) %all-reduce.6.cloned.1.call-update) | async-done | bytes 1048592 | tf_op jit(solution)/shard_map/psum | solution.py:29
  395.6 1.6 constant_dynamic-slice_fusion
  397.2 767.8 %all-reduce.4.cloned.1.call-done = f32[8,8192]{1,0:T(8,128)} async-done(((f32[8,8192]{1,0:T(8,128)}), f32[8,8192]{1,0:T(8,128)}) %all-reduce.4.cloned.1.call-update) | async-done | bytes 262160 | tf_op jit(solution)/shard_map/psum | solution.py:28
  1165.0 1.3 constant_dynamic-slice_fusion.1
  1166.3 474.2 %all-reduce.8.cloned.1.call-done = f32[1024,128]{1,0:T(8,128)} async-done(((f32[1024,128]{1,0:T(8,128)}), f32[1024,128]{1,0:T(8,128)}) %all-reduce.8.cloned.1.call-update) | async-done | bytes 524304 | tf_op jit(solution)/shard_map/psum | solution.py:40
  1640.5 1.9 copy.21
  (9 shorter events, 0.1 us)
Async XLA Ops:
  7.2 1.0 copy-start
  7.2 139.6 %all-gather.2.cloned.1.call-start = ((), (), s32[]{:S(2)}) async-start(), calls=%async_computation | async-start | bytes 1179648 | tf_op jit(solution)/shard_map/all_gather | solution.py:16
  7.9 387.7 %all-reduce.6.cloned.1.call-start = ((), (), s32[]{:S(2)}) async-start(), calls=%async_computation.2 | async-start | bytes 2097152 | tf_op jit(solution)/shard_map/psum | solution.py:29
  8.2 9.7 copy-start.2
  146.5 1018.5 %all-reduce.4.cloned.1.call-start = ((), (), s32[]{:S(2)}) async-start(), calls=%async_computation.1 | async-start | bytes 524288 | tf_op jit(solution)/shard_map/psum | solution.py:28
  166.2 3.9 copy-start.1
  170.0 1470.4 %all-reduce.8.cloned.1.call-start = ((), (), s32[]{:S(2)}) async-start(), calls=%async_computation.3 | async-start | bytes 1048576 | tf_op jit(solution)/shard_map/psum | solution.py:40
Sparse Core Ops, SparseCore 0:
  11.2 95.5 all-gather.1
  146.6 248.9 all-reduce.5
  398.5 766.4 all-reduce.3
  1171.8 468.6 all-reduce.7
where the time goes:
time: 1650 us
  waiting for transfers between devices  1310 us (79%)
  blocking collectives  278 us (17%)
  local copies, waits for them, and re-layouts  37.5 us (2%)
    psum x1, waiting for transfers between devices, local(): left_total = lax.psum(left_part, 'col')  768 us
    psum x1, waiting for transfers between devices, local(): weight_sums = lax.psum((weight_part, bias_part), ('row', 'col'))  474 us
    psum x1, blocking collectives, local(): weight_sums = lax.psum((weight_part, bias_part), ('row', 'col'))  159 us
    all_gather x1, blocking collectives, local(): left = lax.all_gather(side_a, 'col', axis=1, tiled=True).reshape(rows, S, C)  119 us
    psum x1, waiting for transfers between devices, local(): right_total = lax.psum(right_part, 'row')  64.2 us
  transfers between devices with their start and end apart: 4, of which 3 were waited for; matrix products, arithmetic and copies ran while one was open for 3% of the time, Pallas kernels for 0%

commit v1 on v0

--- a/solution.py
+++ b/solution.py
@@ -9,6 +9,11 @@
 
 
 def local(side_a, side_b, pair_grad, out_weight):
+
+    def advance_state(base_x):
+        seen_now = lax.psum(base_x, axis_name="col")
+        return lax.psum(seen_now, axis_name="row")
+
     high = lax.Precision.HIGHEST
     rows = pair_grad.shape[0]
     cols = pair_grad.shape[1]
@@ -37,7 +42,7 @@
     outer = jnp.transpose(outer.reshape(rows, C, cols, C), (0, 2, 1, 3)).reshape(rows * cols, C * C)
     weight_part = jnp.dot(outer.T, flat_pair, precision=high)
     bias_part = jnp.sum(flat_pair, axis=0)
-    weight_sums = lax.psum((weight_part, bias_part), ("row", "col"))
+    weight_sums = advance_state((weight_part, bias_part))
     return (grad_a, grad_b, weight_sums[0], weight_sums[1])
 
 

time: 1650 us -> 1320 us (0.80)
  the two profiles are of different devices: /device:TPU:4 before, /device:TPU:1 now
where the time goes in v1:
time: 1320 us
  waiting for transfers between devices  794 us (60%)
  blocking collectives  455 us (34%)
  local copies, waits for them, and re-layouts  39.2 us (3%)
  matrix products  14.6 us (1%)
  between operations  13.8 us (1%)
    psum x1, waiting for transfers between devices, local(): left_total = lax.psum(left_part, 'col')  793 us
    psum x1, blocking collectives, advance_state(): seen_now = lax.psum(base_x, axis_name='col')  260 us
    all_gather x1, blocking collectives, local(): left = lax.all_gather(side_a, 'col', axis=1, tiled=True).reshape(rows, S, C)  137 us
    psum x1, blocking collectives, advance_state(): return lax.psum(seen_now, axis_name='row')  57.5 us
  transfers between devices with their start and end apart: 3, of which 1 were waited for; matrix products, arithmetic and copies ran while one was open for 2% of the time, Pallas kernels for 0%

profile of v1, /device:TPU:1, one launch (start us, length us, event | category | flops | bytes accessed | tf_op | source)
XLA Modules:
  0.0 1316.5 jit_solution(12140611257966285544)
XLA Ops:
  7.2 0.0 all-gather.2.cloned.1.call-start
  7.2 0.7 all-gather.2.cloned.1.call-update
  7.9 0.0 all-reduce.5.cloned.1.call-start
  8.0 137.4 %all_gather.7 = f32[8,8192]{1,0:T(8,128)S(1)} all-gather(f32[8,128]{1,0:T(8,128)} %param.4), channel_id=1, replica_groups=mesh['row'=8,'col'=64] {'col'}, dimensions={1}, use_global_device_ids=true | all-gather | bytes 266240 | tf_op jit(solution)/shard_map/all_gather | solution.py:20
  145.3 0.3 reshape.53
  145.7 0.3 copy.12
  146.0 5.9 convolution_bitcast_fusion
  151.9 3.7 reshape.48
  155.7 0.0 all-gather.2.cloned.1.call-done
  155.7 3.7 reshape.49
  159.4 2.8 copy.10
  162.2 2.0 convolution_multiply_fusion
  164.3 3.9 reshape.57
  168.2 6.5 copy.17
  174.7 4.6 reshape.58
  179.3 1.0 convolution_multiply_fusion.2
  180.3 0.3 copy.11
  180.7 1.2 reshape.52
  181.9 3.8 fusion.1
  185.7 0.0 all-reduce.5.cloned.1.call-update
  185.8 0.0 all-reduce.7.cloned.1.call-start
  185.8 1.8 convolution_multiply_fusion.1
  187.6 2.6 copy.13
  190.3 4.3 reshape.56
  194.6 793.2 %all-reduce.5.cloned.1.call-done = (f32[8,8192]{1,0:T(8,128)}, f32[1024,128]{1,0:T(8,128)}) async-done(((f32[8,8192]{1,0:T(8,128)}, f32[1024,128]{1,0:T(8,128)}), (f32[8,8192]{1,0:T(8,128)}, f32[1024,128]{1,0:T(8,128)})) %all-reduce.5.cloned.1.call-update) | async-done | bytes 786448 | tf_op jit(solution)/shard_map/psum | solution.py:33
  987.8 0.0 all-reduce.7.cloned.1.call-update
  987.8 0.1 reduce_sum.9
  987.9 259.9 %psum.46 = f32[128]{0:T(128)S(1)} all-reduce(f32[128]{0:T(128)S(1)} %reduce_sum.9), channel_id=1, replica_groups=mesh['row'=8,'col'=64] {'col'}, use_global_device_ids=true, to_apply=%region_5.0 | all-reduce | flops 128 | bytes 1024 | tf_op jit(solution)/shard_map/psum | solution.py:14
  1247.8 57.5 %psum.47 = f32[128]{0:T(128)} all-reduce(f32[128]{0:T(128)S(1)} %psum.46), channel_id=1, replica_groups=mesh['row'=8,'col'=64] {'row'}, use_global_device_ids=true, to_apply=%region_6.0 | all-reduce | flops 128 | bytes 1024 | tf_op jit(solution)/shard_map/psum | solution.py:15
  1305.3 1.3 constant_dynamic-slice_fusion.1
  1306.5 1.6 constant_dynamic-slice_fusion
  1308.1 1.9 copy.22
  (5 shorter events, 0.0 us)
Async XLA Ops:
  7.2 138.8 %copy-start = (f32[1024,128]{1,0:T(8,128)S(1)}, f32[1024,128]{1,0:T(8,128)}, u32[]{:S(2)}) copy-start(f32[1024,128]{1,0:T(8,128)} %param.7) | copy-start | bytes 1572868
  7.2 148.5 %all-gather.2.cloned.1.call-start = ((), (), s32[]{:S(2)}) async-start(), calls=%async_computation | async-start | bytes 1179648 | tf_op jit(solution)/shard_map/all_gather | solution.py:21
  7.9 979.9 %all-reduce.5.cloned.1.call-start = ((), (), s32[]{:S(2)}) async-start(), calls=%async_computation.1 | async-start | bytes 1572864 | tf_op jit(solution)/shard_map/psum | solution.py:33
  174.7 7.2 copy-start.1
  185.8 1120.8 %all-reduce.7.cloned.1.call-start = ((), (), s32[]{:S(2)}) async-start(), calls=%async_computation.2 | async-start | bytes 3145728 | tf_op jit(solution)/shard_map/psum | solution.py:34
Sparse Core Ops, SparseCore 0:
  11.2 95.2 all-gather.1
  185.9 801.8 all-reduce.4
  991.1 307.4 all-reduce.6

commit v2 on v0

--- a/solution.py
+++ b/solution.py
@@ -8,11 +8,18 @@
 P_SIZE = 128
 
 
+def swapped_in(array, name, along):
+    size = lax.axis_size(name)
+    parts = jnp.stack([array for _ in range(size)])
+    parts = lax.all_to_all(parts, name, split_axis=0, concat_axis=0)
+    return jnp.concatenate(parts, axis=along)
+
+
 def local(side_a, side_b, pair_grad, out_weight):
     high = lax.Precision.HIGHEST
     rows = pair_grad.shape[0]
     cols = pair_grad.shape[1]
-    left = lax.all_gather(side_a, "col", axis=1, tiled=True).reshape(rows, S, C)
+    left = swapped_in(side_a, "col", 1).reshape(rows, S, C)
     right = lax.all_gather(side_b, "row", axis=1, tiled=True).reshape(cols, S, C)
     left_flat = jnp.transpose(left, (0, 2, 1)).reshape(rows * C, S)
     right_flat = jnp.transpose(right, (1, 0, 2)).reshape(S, cols * C)

time: 1650 us -> 1590 us (0.964)
  blocking collectives: 278 us -> 133 us
  waiting for transfers between devices: 1310 us -> 1370 us
    all_gather x1 -> x0, blocking collectives: 119 us -> none  [local(): left = lax.all_gather(side_a, 'col', axis=1, tiled=True).reshape(rows, S, C)]
    all_gather x1, waiting for transfers between devices: 0.02 us -> 57.1 us  [local(): lax.all_gather(side_b, 'row', axis=1, tiled=True).reshape(cols, S, C)]
    psum x1, blocking collectives: 159 us -> 133 us  [local(): weight_sums = lax.psum((weight_part, bias_part), ('row', 'col'))]
  transfers between devices with their start and end apart: 4 -> 5, of which waited for: 3 -> 5; matrix products, arithmetic and copies ran while one was open for 3% -> 3% of each run, Pallas kernels for 0% -> 0%
where the time goes in v2:
time: 1590 us
  waiting for transfers between devices  1370 us (86%)
  blocking collectives  133 us (8%)
  local copies, waits for them, and re-layouts  38.6 us (2%)
  starting transfers between devices  16.4 us (1%)
    psum x1, waiting for transfers between devices, local(): left_total = lax.psum(left_part, 'col')  771 us
    psum x1, waiting for transfers between devices, local(): weight_sums = lax.psum((weight_part, bias_part), ('row', 'col'))  474 us
    psum x1, blocking collectives, local(): weight_sums = lax.psum((weight_part, bias_part), ('row', 'col'))  133 us
    psum x1, waiting for transfers between devices, local(): right_total = lax.psum(right_part, 'row')  60.8 us
    all_gather x1, waiting for transfers between devices, local(): lax.all_gather(side_b, 'row', axis=1, tiled=True).reshape(cols, S, C)  57.1 us
  transfers between devices with their start and end apart: 5, of which 5 were waited for; matrix products, arithmetic and copies ran while one was open for 3% of the time, Pallas kernels for 0%

profile of v2, /device:TPU:4, one launch (start us, length us, event | category | flops | bytes accessed | tf_op | source)
XLA Modules:
  0.0 1586.4 jit_solution(7640439222442611940)
XLA Ops:
  7.2 0.7 all-gather.2.cloned.1.call-update
  7.9 1.4 stack.2
  9.3 16.0 %all-to-all-start = ((f32[64,8,128]{2,1,0:T(8,128)}), f32[64,8,128]{2,1,0:T(8,128)S(1)}, u32[]{:S(2)}, u32[]{:S(2)}) async-start(f32[64,8,128]{2,1,0:T(8,128)} %stack.2), calls=%async_computation | async-start | bytes 524288 | tf_op jit(solution)/shard_map/all_to_all | solution.py:14
  25.4 5.9 convolution_bitcast_fusion
  31.4 3.8 reshape.50
  35.2 8.0 all-to-all-done
  43.2 0.1 copy.17
  43.2 0.3 reshape_reshape.3
  43.5 0.3 copy.18
  43.8 1.8 convolution_multiply_fusion.1
  45.6 2.6 copy.19
  48.3 4.4 reshape.58
  52.7 0.2 all-reduce.4.cloned.1.call-start
  52.9 57.1 %all-gather.2.cloned.1.call-done = f32[32,8192]{1,0:T(8,128)} async-done(((f32[32,1024]{1,0:T(8,128)}), f32[32,8192]{1,0:T(8,128)}) %all-gather.2.cloned.1.call-update) | async-done | bytes 1048592 | tf_op jit(solution)/shard_map/all_gather | solution.py:23
  110.0 3.7 reshape.51
  113.7 2.8 copy.15
  116.5 1.0 convolution_multiply_fusion.2
  117.5 0.3 copy.16
  117.9 1.2 reshape.54
  119.1 1.0 convolution_multiply_fusion
  120.1 2.7 reshape.59
  122.8 6.5 copy.23
  129.4 3.8 reshape.60
  133.2 2.6 fusion.1
  135.9 0.1 reduce_sum.9
  135.9 133.3 %psum.31 = f32[128]{0:T(128)} all-reduce(f32[128]{0:T(128)S(1)} %reduce_sum.9), channel_id=1, replica_groups=mesh['row'=8,'col'=64] {'row','col'}, use_global_device_ids=true, to_apply=%region_4.0 | all-reduce | flops 128 | bytes 1024 | tf_op jit(solution)/shard_map/psum | solution.py:47
  269.2 60.8 %all-reduce.6.cloned.1.call-done = f32[32,8192]{1,0:T(8,128)} async-done(((f32[32,8192]{1,0:T(8,128)}), f32[32,8192]{1,0:T(8,128)}) %all-reduce.6.cloned.1.call-update) | async-done | bytes 1048592 | tf_op jit(solution)/shard_map/psum | solution.py:36
  329.9 1.6 constant_dynamic-slice_fusion
  331.5 771.0 %all-reduce.4.cloned.1.call-done = f32[8,8192]{1,0:T(8,128)} async-done(((f32[8,8192]{1,0:T(8,128)}), f32[8,8192]{1,0:T(8,128)}) %all-reduce.4.cloned.1.call-update) | async-done | bytes 262160 | tf_op jit(solution)/shard_map/psum | solution.py:35
  1102.5 1.3 constant_dynamic-slice_fusion.1
  1103.8 474.2 %all-reduce.8.cloned.1.call-done = f32[1024,128]{1,0:T(8,128)} async-done(((f32[1024,128]{1,0:T(8,128)}), f32[1024,128]{1,0:T(8,128)}) %all-reduce.8.cloned.1.call-update) | async-done | bytes 524304 | tf_op jit(solution)/shard_map/psum | solution.py:47
  1578.0 1.9 copy.27
  (10 shorter events, 0.2 us)
Async XLA Ops:
  7.2 18.3 %copy-start = (f32[1024,128]{1,0:T(8,128)S(1)}, f32[1024,128]{1,0:T(8,128)}, u32[]{:S(2)}) copy-start(f32[1024,128]{1,0:T(8,128)} %param.7) | copy-start | bytes 1572868
  7.2 102.8 %all-gather.2.cloned.1.call-start = ((), (), s32[]{:S(2)}) async-start(), calls=%async_computation.1 | async-start | bytes 1179648 | tf_op jit(solution)/shard_map/all_gather | solution.py:23
  9.3 33.8 %all-to-all-start = ((f32[64,8,128]{2,1,0:T(8,128)}), f32[64,8,128]{2,1,0:T(8,128)S(1)}, u32[]{:S(2)}, u32[]{:S(2)}) async-start(f32[64,8,128]{2,1,0:T(8,128)} %stack.2), calls=%async_computation | async-start | bytes 524288 | tf_op jit(solution)/shard_map/all_to_all | solution.py:14
  25.4 304.6 %all-reduce.6.cloned.1.call-start = ((), (), s32[]{:S(2)}) async-start(), calls=%async_computation.3 | async-start | bytes 2097152 | tf_op jit(solution)/shard_map/psum | solution.py:36
  52.7 1049.9 %all-reduce.4.cloned.1.call-start = ((), (), s32[]{:S(2)}) async-start(), calls=%async_computation.2 | async-start | bytes 524288 | tf_op jit(solution)/shard_map/psum | solution.py:35
  129.4 3.9 copy-start.1
  133.2 1444.8 %all-reduce.8.cloned.1.call-start = ((), (), s32[]{:S(2)}) async-start(), calls=%async_computation.4 | async-start | bytes 1048576 | tf_op jit(solution)/shard_map/psum | solution.py:47
Sparse Core Ops, SparseCore 0:
  11.2 98.6 all-gather.1
  112.9 216.9 all-reduce.5
  332.9 769.6 all-reduce.3
  1109.3 468.6 all-reduce.7

commit v3 on v0

--- a/solution.py
+++ b/solution.py
@@ -25,7 +25,8 @@
     left_part = jnp.transpose(left_grad.reshape(rows, C, S), (0, 2, 1)).reshape(rows, S * C)
     right_grad = jnp.dot(left_flat.T, grad_tile, precision=high) / S
     right_part = jnp.transpose(right_grad.reshape(S, cols, C), (1, 0, 2)).reshape(cols, S * C)
-    left_total = lax.psum(left_part, "col")
+    parts = lax.all_gather(left_part, "col")
+    left_total = jnp.sum(parts, axis=0)
     right_total = lax.psum(right_part, "row")
     left_width = side_a.shape[1]
     right_width = side_b.shape[1]

time: 1650 us -> 1000 us (0.61)
  waiting for transfers between devices: 1310 us -> 652 us
    psum x1 -> x0, waiting for transfers between devices: 768 us -> none  [local(): left_total = lax.psum(left_part, 'col')]
    all_gather x0 -> x1, waiting for transfers between devices: none -> 135 us  [local(): parts = lax.all_gather(left_part, 'col')]
    psum x1, waiting for transfers between devices: 474 us -> 455 us  [local(): weight_sums = lax.psum((weight_part, bias_part), ('row', 'col'))]
  transfers between devices with their start and end apart: 4 -> 4, of which waited for: 3 -> 3; matrix products, arithmetic and copies ran while one was open for 3% -> 5% of each run, Pallas kernels for 0% -> 0%
where the time goes in v3:
time: 1000 us
  waiting for transfers between devices  652 us (65%)
  blocking collectives  278 us (28%)
  local copies, waits for them, and re-layouts  36.8 us (4%)
  between operations  13.9 us (1%)
  matrix products  12.4 us (1%)
    psum x1, waiting for transfers between devices, local(): weight_sums = lax.psum((weight_part, bias_part), ('row', 'col'))  455 us
    psum x1, blocking collectives, local(): weight_sums = lax.psum((weight_part, bias_part), ('row', 'col'))  159 us
    all_gather x1, waiting for transfers between devices, local(): parts = lax.all_gather(left_part, 'col')  135 us
    all_gather x1, blocking collectives, local(): left = lax.all_gather(side_a, 'col', axis=1, tiled=True).reshape(rows, S, C)  119 us
    psum x1, waiting for transfers between devices, local(): right_total = lax.psum(right_part, 'row')  61.9 us
  transfers between devices with their start and end apart: 4, of which 3 were waited for; matrix products, arithmetic and copies ran while one was open for 5% of the time, Pallas kernels for 0%

profile of v3, /device:TPU:4, one launch (start us, length us, event | category | flops | bytes accessed | tf_op | source)
XLA Modules:
  0.0 1000.8 jit_solution(6339201219841638219)
XLA Ops:
  7.2 0.7 all-gather.3.cloned.1.call-update
  7.9 0.0 all-reduce.3.cloned.1.call-start
  8.0 0.3 copy-done
  8.2 5.9 convolution_bitcast_fusion
  14.1 3.7 reshape.45
  17.9 119.1 %all_gather.11 = f32[8,8192]{1,0:T(8,128)S(1)} all-gather(f32[8,128]{1,0:T(8,128)S(1)} %copy-done.2), channel_id=1, replica_groups=mesh['row'=8,'col'=64] {'col'}, dimensions={1}, use_global_device_ids=true | all-gather | bytes 266240 | tf_op jit(solution)/shard_map/all_gather | solution.py:15
  137.0 0.3 reshape.49
  137.3 0.3 copy.16
  137.6 1.8 convolution_multiply_fusion.1
  139.5 2.6 copy.17
  142.1 4.4 reshape.52
  146.5 0.0 all-gather.5.cloned.1.call-start
  146.6 3.7 reshape.46
  150.3 2.8 copy.14
  153.1 1.0 convolution_multiply_fusion.2
  154.2 0.3 copy.15
  154.5 1.2 all_gather_reshape.3
  155.8 0.2 all-reduce.5.cloned.1.call-start
  156.0 1.0 convolution_multiply_fusion
  157.1 2.7 reshape.53
  159.8 6.5 copy.21
  166.3 3.8 reshape.54
  170.1 2.6 fusion.1
  172.7 0.1 reduce_sum.19
  172.8 159.4 %psum.23 = f32[128]{0:T(128)} all-reduce(f32[128]{0:T(128)S(1)} %reduce_sum.19), channel_id=1, replica_groups=mesh['row'=8,'col'=64] {'row','col'}, use_global_device_ids=true, to_apply=%region_4.0 | all-reduce | flops 128 | bytes 1024 | tf_op jit(solution)/shard_map/psum | solution.py:41
  332.2 61.9 %all-reduce.3.cloned.1.call-done = f32[32,8192]{1,0:T(8,128)} async-done(((f32[32,8192]{1,0:T(8,128)}), f32[32,8192]{1,0:T(8,128)}) %all-reduce.3.cloned.1.call-update) | async-done | bytes 1048592 | tf_op jit(solution)/shard_map/psum | solution.py:30
  394.1 1.6 constant_dynamic-slice_fusion
  395.6 134.9 %all-gather.5.cloned.1.call-done = f32[64,8,8192]{2,1,0:T(8,128)} async-done(((f32[1,8,8192]{2,1,0:T(8,128)}), f32[64,8,8192]{2,1,0:T(8,128)}) %all-gather.5.cloned.1.call-update) | async-done | bytes 16777232 | tf_op jit(solution)/shard_map/all_gather | solution.py:28
  530.6 6.5 reduce_sum.18
  537.1 0.6 constant_dynamic-slice_fusion.1
  537.7 454.7 %all-reduce.5.cloned.1.call-done = f32[1024,128]{1,0:T(8,128)} async-done(((f32[1024,128]{1,0:T(8,128)}), f32[1024,128]{1,0:T(8,128)}) %all-reduce.5.cloned.1.call-update) | async-done | bytes 524304 | tf_op jit(solution)/shard_map/psum | solution.py:41
  992.4 1.9 copy.24
  (10 shorter events, 0.1 us)
Async XLA Ops:
  7.2 1.0 copy-start
  7.2 139.4 %all-gather.3.cloned.1.call-start = ((), (), s32[]{:S(2)}) async-start(), calls=%async_computation | async-start | bytes 1179648 | tf_op jit(solution)/shard_map/all_gather | solution.py:16
  7.9 386.2 %all-reduce.3.cloned.1.call-start = ((), (), s32[]{:S(2)}) async-start(), calls=%async_computation.2 | async-start | bytes 2097152 | tf_op jit(solution)/shard_map/psum | solution.py:30
  8.2 9.7 copy-start.2
  146.5 384.1 %all-gather.5.cloned.1.call-start = ((), (), s32[]{:S(2)}) async-start(), calls=%async_computation.1 | async-start | bytes 17039360 | tf_op jit(solution)/shard_map/all_gather | solution.py:28
  155.8 836.7 %all-reduce.5.cloned.1.call-start = ((), (), s32[]{:S(2)}) async-start(), calls=%async_computation.3 | async-start | bytes 1048576 | tf_op jit(solution)/shard_map/psum | solution.py:41
  166.3 3.8 copy-start.1
Sparse Core Ops, SparseCore 0:
  11.2 95.5 all-gather.2
  146.6 247.3 all-reduce.2
  396.2 134.2 all-gather.4
  536.5 455.9 all-reduce.4
